TPU v7x, 32 devices: a whole 2x2x4 slice. The times are simulated.
32 devices in a mesh: seq: 16 (over z, y, x), head: 2 (over core).
Axes of the slice: x: 2, y: 2, z: 4, core: 2. Of those that a mesh axis runs over, the one named last changes fastest.
Arguments:
- q_lin: bfloat16 [4096, 512], P('seq', 'head'), may hold values from -6 to 6
- k_lin: bfloat16 [4096, 512], P('seq', 'head'), may hold values from -6 to 6
- v_lin: bfloat16 [4096, 512], P('seq', 'head'), may hold values from -6 to 6
- log_decay: float32 [4, 4096], P('head', 'seq'), may hold values from -0.4 to 0, as said below
- q_soft: bfloat16 [4096, 512], P('seq', 'head'), may hold values from -12 to 12
- k_soft: bfloat16 [4096, 512], P('seq', 'head'), may hold values from -6 to 6
- v_soft: bfloat16 [4096, 512], P('seq', 'head'), may hold values from -6 to 6
- wo_lin: bfloat16 [512, 4096], P('head'), may hold values from -0.375 to 0.375
- wo_soft: bfloat16 [512, 4096], P('head'), may hold values from -0.375 to 0.375
Outputs:
- lin_mixed: bfloat16 [4096, 4096], P('seq', 'head')
- soft_mixed: bfloat16 [4096, 4096], P('seq', 'head')
Inputs may be any that keep to these rules, and one draw needn't show every extreme that they name: `log_decay`: log decays are never positive.
All inputs are finite; a program needn't handle non-finite values.
Results may differ from a plain program's by a relative error of at most 0.012.
Values may be sent and summed in bfloat16 or wider, within the bound.
A program may use at most 64 MiB of HBM per device.

v0:
```python
import math
import jax
import jax.numpy as jnp
from jax import lax
from jax.sharding import PartitionSpec as P

HIGHEST = lax.Precision.HIGHEST
NEG_BIG = -1e30


def prefix(shard, axis, combine, identity):
    size, here = (lax.axis_size(axis), lax.axis_index(axis))
    everything = jax.tree.map(
        lambda part, kind: lax.all_gather(part.astype(kind), axis),
        shard,
        (jnp.bfloat16, jnp.bfloat16),
    )
    start = jax.tree.map(
        lambda part, zero: jnp.broadcast_to(jnp.asarray(zero, part.dtype), part.shape),
        shard,
        identity,
    )

    def turn(k, before):
        reached = k < here
        new = combine(
            before, jax.tree.map(lambda part, own: part[k].astype(own.dtype), everything, shard)
        )
        return jax.tree.map(lambda a, b: jnp.where(reached, a, b), new, before)

    return lax.fori_loop(0, size, turn, start)


def second_half(device):
    return 2 * device + 1


def absorb(state, query_half, key_block, value_block, allowed, factor):
    row_top, row_sum, weighted = state
    scores = (
        jnp.einsum("qhd,khd->hqk", query_half, key_block, preferred_element_type=jnp.float32)
        * factor
    )
    if allowed is not None:
        scores = jnp.where(allowed[None], scores, -jnp.inf)
    new_top = jnp.maximum(row_top, jnp.max(scores, axis=-1))
    shrink = jnp.exp(row_top - new_top)
    weights = jnp.exp(scores - new_top[:, :, None])
    row_sum = row_sum * shrink + jnp.sum(weights, axis=-1)
    weighted = weighted * shrink.T[:, :, None] + jnp.einsum(
        "hqk,khd->qhd",
        weights.astype(jnp.bfloat16),
        value_block,
        preferred_element_type=jnp.float32,
    )
    return (new_top, row_sum, weighted)


def lightning_heads(q_lin, k_lin, v_lin, log_decay):
    row_count = q_lin.shape[0]
    head_count = log_decay.shape[0]
    head_width = q_lin.shape[1] // head_count
    query_plain = q_lin.reshape(row_count, head_count, head_width)
    key_plain = k_lin.reshape(row_count, head_count, head_width)
    queries = query_plain.astype(jnp.float32)
    key_rows = key_plain.astype(jnp.float32)
    values = v_lin.astype(jnp.float32).reshape(row_count, head_count, head_width)
    cumulative = jnp.cumsum(log_decay, axis=1)
    lower = jnp.arange(row_count)[:, None] >= jnp.arange(row_count)[None, :]
    decay_gap = jnp.where(lower[None], cumulative[:, :, None] - cumulative[:, None, :], -jnp.inf)
    scores = jnp.einsum(
        "thd,shd->hts", query_plain, key_plain, preferred_element_type=jnp.float32
    ) * jnp.exp(decay_gap)
    inside = jnp.einsum("hts,shd->thd", scores, values, precision=HIGHEST)
    closing = jnp.exp(cumulative[:, -1:] - cumulative)
    own_state = jnp.einsum(
        "shd,she->hde", key_rows * closing.T[:, :, None], values, precision=HIGHEST
    )
    own_decay = cumulative[:, -1]

    def combine(earlier, later):
        return (jnp.exp(later[1])[:, None, None] * earlier[0] + later[0], earlier[1] + later[1])

    identity = (jnp.zeros_like(own_state), jnp.zeros_like(own_decay))
    carried, _ = prefix((own_state, own_decay), "seq", combine, identity)
    from_before = (
        jnp.einsum("thd,hde->the", queries, carried, precision=HIGHEST)
        * jnp.exp(cumulative).T[:, :, None]
    )
    raw = inside + from_before
    factor = lax.rsqrt(jnp.mean(raw * raw, axis=-1, keepdims=True) + 1e-06)
    return (raw * factor).astype(jnp.bfloat16).reshape(row_count, head_count * head_width)


def softmax_heads(q_soft, k_soft, v_soft, head_width):
    row_count = q_soft.shape[0]
    half_rows = row_count // 2
    head_count = q_soft.shape[1] // head_width
    own_index = lax.axis_index("seq")
    factor = 1.0 / math.sqrt(head_width)
    shaped = q_soft.reshape(2, half_rows, head_count, head_width)
    query_ids = (2 * own_index, second_half(own_index))
    triangle = jnp.arange(half_rows)[:, None] >= jnp.arange(half_rows)[None, :]

    def block_pass(state, side, key_block, value_block, key_id):

        def full_block(inner_state):
            return absorb(inner_state, shaped[side], key_block, value_block, None, factor)

        def diagonal_block(inner_state):
            return absorb(inner_state, shaped[side], key_block, value_block, triangle, factor)

        def skipped(inner_state):
            return inner_state

        def not_below(inner_state):
            return lax.cond(key_id == query_ids[side], diagonal_block, skipped, inner_state)

        return lax.cond(key_id < query_ids[side], full_block, not_below, state)

    start_state = tuple(
        (
            (
                jnp.full((head_count, half_rows), NEG_BIG, jnp.float32),
                jnp.zeros((head_count, half_rows), jnp.float32),
                jnp.zeros((half_rows, head_count, head_width), jnp.float32),
            )
            for side in range(2)
        )
    )
    carry = start_state
    key_piece = lax.all_gather(k_soft, "seq", axis=0, tiled=True)
    value_piece = lax.all_gather(v_soft, "seq", axis=0, tiled=True)
    piece_rows = key_piece.shape[0]
    blocks = piece_rows // half_rows
    key_blocks = key_piece.reshape(blocks, half_rows, head_count, head_width)
    value_blocks = value_piece.reshape(blocks, half_rows, head_count, head_width)
    firsts = half_rows * jnp.arange(blocks, dtype=jnp.int32)

    def inner(state, block_item):
        key_block, value_block, first = block_item
        key_id = first // half_rows
        return (
            tuple(
                (block_pass(state[side], side, key_block, value_block, key_id) for side in range(2))
            ),
            None,
        )

    carry, _ = lax.scan(inner, carry, (key_blocks, value_blocks, firsts))
    halves = [
        (carry[side][2] / carry[side][1].T[:, :, None])
        .astype(jnp.bfloat16)
        .reshape(half_rows, head_count * head_width)
        for side in range(2)
    ]
    return jnp.concatenate(halves, axis=0)


def local(q_lin, k_lin, v_lin, log_decay, q_soft, k_soft, v_soft, wo_lin, wo_soft):
    head_width = q_lin.shape[1] // log_decay.shape[0]
    lin_out = lightning_heads(q_lin, k_lin, v_lin, log_decay)
    soft_out = softmax_heads(q_soft, k_soft, v_soft, head_width)
    lin_term = jnp.dot(lin_out, wo_lin, preferred_element_type=jnp.float32)
    soft_term = jnp.dot(soft_out, wo_soft, preferred_element_type=jnp.float32)
    lin_sum, soft_sum = (
        lax.psum_scatter(
            lin_term.astype(jnp.bfloat16).astype(jnp.float32).astype(jnp.bfloat16),
            "head",
            scatter_dimension=1,
            tiled=True,
        ).astype(jnp.float32),
        lax.psum_scatter(
            soft_term.astype(jnp.bfloat16).astype(jnp.float32).astype(jnp.bfloat16),
            "head",
            scatter_dimension=1,
            tiled=True,
        ).astype(jnp.float32),
    )
    return (lin_sum.astype(jnp.bfloat16), soft_sum.astype(jnp.bfloat16))


def solution(mesh):
    in_specs = (
        P("seq", "head"),
        P("seq", "head"),
        P("seq", "head"),
        P("head", "seq"),
        P("seq", "head"),
        P("seq", "head"),
        P("seq", "head"),
        P("head", None),
        P("head", None),
    )
    out_specs = (P("seq", "head"), P("seq", "head"))
    return jax.shard_map(local, mesh=mesh, in_specs=in_specs, out_specs=out_specs, check_vma=False)
```

profile of v0, /device:TPU:0, one launch (start us, length us, event | category | flops | bytes accessed | tf_op | source)
XLA Modules:
  0.0 389.1 jit_solution(17133437121583700277)
XLA Ops:
  9.3 1.0 copy.69
  10.4 1.8 convolution_convert_fusion.2
  13.8 1.2 dynamic-slice
  15.9 43.7 %all-reduce = bf16[32]{0:T(256)(128)(2,1)S(1)} all-reduce(bf16[32]{0:T(256)(128)(2,1)S(1)} %dynamic-update-slice), channel_id=2, replica_groups=mesh['seq'=16,'head'=2] {'seq'}, use_global_device_ids=true, to_apply=%add | all-reduce | flops 32 | bytes 128
  59.7 1.0 reshape.130
  60.7 1.1 convolution_multiply_fusion.4
  61.8 8.6 %all-gather.10.cloned.1.call-done = bf16[32,128,128]{2,1,0:T(8,128)(2,1)} async-done(((bf16[2,128,128]{2,1,0:T(8,128)(2,1)}), bf16[32,128,128]{2,1,0:T(8,128)(2,1)}) %all-gather.10.cloned.1.call-update) | async-done | bytes 1048592 | tf_op jit(solution)/shard_map/all_gather | solution.py:14
  70.5 15.6 %while.39 = (s32[]{:T(128)}, f32[2,128,128]{2,1,0:T(8,128)S(1)}, s32[]{:T(128)}, bf16[16,2]{1,0:T(8,128)(2,1)S(1)}, bf16[16,2,128,128]{3,2,1,0:T(8,128)(2,1)}, /*index=5*/s32[]{:T(128)}, s32[]{:T(128)}) while((s32[]{:T(128)}, f32[2,128,128]{2,1,0:T(8,128)S(1)}, s32[]{:T(128)}, bf16[16,2]{1,0:T(8,128)(2,1)S(1)}, ...), condition=%wide.region_3.4_spmd.clone, body=%wide.region_2.3_spmd.clone.sunk | while | flops 163846 | bytes 327813 | solution.py:31
  70.5 0.9 fusion.77
  71.5 0.9 fusion.77
  72.4 0.9 fusion.77
  73.4 0.9 fusion.77
  74.4 0.9 fusion.77
  75.4 0.9 fusion.77
  76.3 0.9 fusion.77
  77.3 0.9 fusion.77
  78.3 0.9 fusion.77
  79.3 0.9 fusion.77
  80.2 0.9 fusion.77
  81.2 0.9 fusion.77
  82.2 0.9 fusion.77
  83.2 0.9 fusion.77
  84.1 0.9 fusion.77
  85.1 0.9 fusion.77
  86.9 2.1 convolution_convert_fusion.1
  89.1 43.7 %all-gather.6.cloned.1.call-done = bf16[4096,256]{1,0:T(8,128)(2,1)} async-done(((bf16[256,256]{1,0:T(8,128)(2,1)}), bf16[4096,256]{1,0:T(8,128)(2,1)}) %all-gather.6.cloned.1.call-update) | async-done | bytes 2097168 | tf_op jit(solution)/shard_map/all_gather | solution.py:132
  132.8 4.0 %reshape.143 = bf16[32,128,2,128]{3,2,1,0:T(2,128)(2,1)} reshape(bf16[4096,256]{1,0:T(8,128)(2,1)} %all-gather.6.cloned.1.call-done) | data formatting | bytes 4194304 | tf_op jit(solution)/shard_map/reshape | solution.py:136
  136.8 58.2 %all-gather.8.cloned.1.call-done = bf16[4096,256]{1,0:T(8,128)(2,1)} async-done(((bf16[256,256]{1,0:T(8,128)(2,1)}), bf16[4096,256]{1,0:T(8,128)(2,1)}) %all-gather.8.cloned.1.call-update) | async-done | bytes 2097168 | tf_op jit(solution)/shard_map/all_gather | solution.py:133
  195.0 4.0 %reshape.144 = bf16[32,128,2,128]{3,2,1,0:T(2,128)(2,1)} reshape(bf16[4096,256]{1,0:T(8,128)(2,1)} %all-gather.8.cloned.1.call-done) | data formatting | bytes 4194304 | tf_op jit(solution)/shard_map/reshape | solution.py:137
  199.0 141.2 %while.38 = (s32[]{:T(128)}, f32[2,128]{1,0:T(2,128)S(1)}, f32[2,128]{1,0:T(2,128)S(1)}, f32[128,2,128]{2,0,1:T(8,128)S(1)}, f32[2,128]{1,0:T(2,128)S(1)}, /*ind...) while((s32[]{:T(128)}, f32[2,128]{1,0:T(2,128)S(1)}, ...), condition=%wide.region_23.24_spmd.clone.clone, body=%wide.region_6.23_spmd.clone.clone.sunk | while | flops 34162200 | bytes 2311003 | solution.py:150
  202.3 1.0 constant_dynamic-slice_fusion.3
  207.7 1.0 constant_dynamic-slice_fusion.3
  212.6 1.0 constant_dynamic-slice_fusion.3
  216.9 1.0 constant_dynamic-slice_fusion.3
  221.3 1.0 constant_dynamic-slice_fusion.3
  225.7 1.0 constant_dynamic-slice_fusion.3
  230.0 1.0 constant_dynamic-slice_fusion.3
  234.4 1.0 constant_dynamic-slice_fusion.3
  238.7 1.0 constant_dynamic-slice_fusion.3
  243.1 1.0 constant_dynamic-slice_fusion.3
  247.5 1.0 constant_dynamic-slice_fusion.3
  251.8 1.0 constant_dynamic-slice_fusion.3
  256.2 1.0 constant_dynamic-slice_fusion.3
  260.5 1.0 constant_dynamic-slice_fusion.3
  264.9 1.0 constant_dynamic-slice_fusion.3
  269.3 1.0 constant_dynamic-slice_fusion.3
  273.6 1.0 constant_dynamic-slice_fusion.3
  278.0 1.0 constant_dynamic-slice_fusion.3
  282.4 1.0 constant_dynamic-slice_fusion.3
  286.7 1.0 constant_dynamic-slice_fusion.3
  291.1 1.0 constant_dynamic-slice_fusion.3
  295.4 1.0 constant_dynamic-slice_fusion.3
  299.8 1.0 constant_dynamic-slice_fusion.3
  304.2 1.0 constant_dynamic-slice_fusion.3
  308.5 1.0 constant_dynamic-slice_fusion.3
  312.9 1.0 constant_dynamic-slice_fusion.3
  317.2 1.0 constant_dynamic-slice_fusion.3
  321.6 1.0 constant_dynamic-slice_fusion.3
  326.0 1.0 constant_dynamic-slice_fusion.3
  330.3 1.0 constant_dynamic-slice_fusion.3
  334.7 1.0 constant_dynamic-slice_fusion.3
  339.1 1.0 constant_dynamic-slice_fusion.3
  340.4 3.6 convolution_convert_fusion
  344.1 38.5 %reduce-scatter.5.cloned.1.call-done = bf16[256,2048]{1,0:T(8,128)(2,1)} async-done(((bf16[256,4096]{1,0:T(8,128)(2,1)}), bf16[256,2048]{1,0:T(8,128)(2,1)}) %reduce-scatter.5.cloned.1.call-update) | async-done | bytes 1048592 | tf_op jit(solution)/shard_map/reduce_scatter | solution.py:173
  (337 shorter events, 33.2 us)
Async XLA Ops:
  7.2 79.8 %copy-start = (bf16[256,4096]{1,0:T(8,128)(2,1)S(1)}, bf16[256,4096]{1,0:T(8,128)(2,1)}, u32[]{:S(2)}) copy-start(bf16[256,4096]{1,0:T(8,128)(2,1)} %param.28) | copy-start | bytes 6291460
  7.2 63.3 %all-gather.10.cloned.1.call-start = ((), (), s32[]{:S(2)}) async-start(), calls=%async_computation.6 | async-start | bytes 1114112 | tf_op jit(solution)/shard_map/all_gather | solution.py:14
  10.3 75.7 %copy-start.2 = (bf16[256,256]{1,0:T(8,128)(2,1)S(1)}, bf16[256,256]{1,0:T(8,128)(2,1)}, u32[]{:S(2)}) copy-start(bf16[256,256]{1,0:T(8,128)(2,1)} %param.21) | copy-start | bytes 393220
  12.2 120.6 %all-gather.6.cloned.1.call-start = ((), (), s32[]{:S(2)}) async-start(), calls=%async_computation.3 | async-start | bytes 2228224 | tf_op jit(solution)/shard_map/all_gather | solution.py:132
  13.0 73.4 %copy-start.1 = (bf16[256,256]{1,0:T(8,128)(2,1)S(1)}, bf16[256,256]{1,0:T(8,128)(2,1)}, u32[]{:S(2)}) copy-start(bf16[256,256]{1,0:T(8,128)(2,1)} %param.23) | copy-start | bytes 393220
  13.0 182.0 %all-gather.8.cloned.1.call-start = ((), (), s32[]{:S(2)}) async-start(), calls=%async_computation.4 | async-start | bytes 2228224 | tf_op jit(solution)/shard_map/all_gather | solution.py:133
  13.7 330.4 %reduce-scatter.3.cloned.1.call-start = ((), (), s32[]{:S(2)}) async-start(), calls=%async_computation.2 | async-start | bytes 3145728 | tf_op jit(solution)/shard_map/reduce_scatter | solution.py:167
  89.0 293.5 %reduce-scatter.5.cloned.1.call-start = ((), (), s32[]{:S(2)}) async-start(), calls=%async_computation.5 | async-start | bytes 3145728 | tf_op jit(solution)/shard_map/reduce_scatter | solution.py:173
Sparse Core Ops, SparseCore 0:
  12.3 58.0 all-gather.9
  73.2 59.5 all-gather.5
  135.6 59.3 all-gather.7
  197.6 8.2 reduce-scatter.2
  344.2 38.3 reduce-scatter.4
where the time goes:
time: 393 us; the launch traced here: 389 us
  waiting for transfers between devices  150 us (38%)
  loops' own time  89.1 us (23%)
  local copies, waits for them, and re-layouts  63.5 us (16%)
  blocking collectives  43.7 us (11%)
  other arithmetic  16.9 us (4%)
  between operations  14.6 us (4%)
  matrix products  10.7 us (3%)
    another operation x1, loops' own time, softmax_heads(): carry, _ = lax.scan(inner, carry, (key_blocks, value_blocks, firsts))  85.6 us
    all_gather x1, waiting for transfers between devices, softmax_heads(): value_piece = lax.all_gather(v_soft, 'seq', axis=0, tiled=True)  58.2 us
    dynamic_slice x128, local copies, waits for them, and re-layouts, softmax_heads(): carry, _ = lax.scan(inner, carry, (key_blocks, value_blocks, firsts))  50.6 us
    all_gather x1, waiting for transfers between devices, softmax_heads(): key_piece = lax.all_gather(k_soft, 'seq', axis=0, tiled=True)  43.7 us
    unnamed x1, blocking collectives  43.7 us
    reduce_scatter x1, waiting for transfers between devices, local(): lax.psum_scatter(soft_term.astype(jnp.bfloat16).astype(jnp.float32).astyp...  38.5 us
    select_n x16, other arithmetic, turn(): return jax.tree.map(lambda a, b: jnp.where(reached, a, b), new, before)  14.9 us
    all_gather x1, waiting for transfers between devices, prefix(): lax.all_gather(part.astype(kind), axis)  8.65 us
  transfers between devices with their start and end apart: 5, of which 4 were waited for; matrix products, arithmetic and copies ran while one was open for 22% of the time, Pallas kernels for 0%

commit v1 on v0

--- a/solution.py
+++ b/solution.py
@@ -6,6 +6,26 @@
 
 HIGHEST = lax.Precision.HIGHEST
 NEG_BIG = -1e30
+
+
+def work_racks(local_x, dim_at):
+    local_x = jnp.moveaxis(local_x, 0, dim_at)
+    q_next = local_x.shape
+    return local_x.reshape(
+        *q_next[:dim_at], q_next[dim_at] * q_next[dim_at + 1], *q_next[dim_at + 2 :]
+    )
+
+
+def time_stops_all(inputs, axis_key, array_dim):
+    many = lax.axis_size(axis_key)
+    items = [(pp, (pp + 1) % many) for pp in range(many)]
+    seen = [inputs]
+    while len(seen) < many:
+        seen.append(lax.ppermute(seen[-1], axis_key, perm=items))
+    fresh = lax.axis_index(axis_key)
+    work_now = jnp.stack(seen)
+    seen = work_now[(fresh - jnp.arange(many)) % many]
+    return work_racks(seen, array_dim)
 
 
 def prefix(shard, axis, combine, identity):
@@ -130,7 +150,7 @@
     )
     carry = start_state
     key_piece = lax.all_gather(k_soft, "seq", axis=0, tiled=True)
-    value_piece = lax.all_gather(v_soft, "seq", axis=0, tiled=True)
+    value_piece = time_stops_all(v_soft, "seq", 0)
     piece_rows = key_piece.shape[0]
     blocks = piece_rows // half_rows
     key_blocks = key_piece.reshape(blocks, half_rows, head_count, head_width)

time: 393 us -> 414 us (1.053)
  local copies, waits for them, and re-layouts: 63.5 us -> 77.2 us
  waiting for transfers between devices: 150 us -> 156 us
    ppermute x0 -> x15, waiting for transfers between devices: none -> 121 us  [time_stops_all(): seen.append(lax.ppermute(seen[-1], axis_key, perm=items))]
    all_gather x1 -> x0, waiting for transfers between devices: 58.2 us -> none  [softmax_heads(): value_piece = lax.all_gather(v_soft, 'seq', axis=0, tiled=True)]
    all_gather x1, waiting for transfers between devices: 43.7 us -> 0.02 us  [softmax_heads(): key_piece = lax.all_gather(k_soft, 'seq', axis=0, tiled=True)]
    unnamed x12 -> x31, local copies, waits for them, and re-layouts: 1.61 us -> 11.9 us
    all_gather x1, waiting for transfers between devices: 8.65 us -> 0.01 us  [prefix(): lax.all_gather(part.astype(kind), axis)]
    another operation x6 -> x8, local copies, waits for them, and re-layouts: 0.03 us -> 4.68 us  [the longest x1 3.99 us: softmax_heads(): value_piece.reshape(blocks, half_rows, head_count, head_width)]
  transfers between devices with their start and end apart: 5 -> 19, of which waited for: 4 -> 15; matrix products, arithmetic and copies ran while one was open for 22% -> 24% of each run, Pallas kernels for 0% -> 0%
where the time goes in v1:
time: 414 us; the launch traced here: 410 us
  waiting for transfers between devices  156 us (38%)
  loops' own time  89 us (21%)
  local copies, waits for them, and re-layouts  77.2 us (19%)
  blocking collectives  41.6 us (10%)
  other arithmetic  16.9 us (4%)
  between operations  14.7 us (4%)
  matrix products  10.7 us (3%)
    ppermute x15, waiting for transfers between devices, time_stops_all(): seen.append(lax.ppermute(seen[-1], axis_key, perm=items))  121 us
    another operation x1, loops' own time, softmax_heads(): carry, _ = lax.scan(inner, carry, (key_blocks, value_blocks, firsts))  85.7 us
    dynamic_slice x128, local copies, waits for them, and re-layouts, softmax_heads(): carry, _ = lax.scan(inner, carry, (key_blocks, value_blocks, firsts))  50.6 us
    unnamed x1, blocking collectives  41.6 us
    reduce_scatter x1, waiting for transfers between devices, local(): lax.psum_scatter(soft_term.astype(jnp.bfloat16).astype(jnp.float32).astyp...  35.3 us
    select_n x16, other arithmetic, turn(): return jax.tree.map(lambda a, b: jnp.where(reached, a, b), new, before)  14.9 us
    unnamed x31, local copies, waits for them, and re-layouts  11.9 us
  transfers between devices with their start and end apart: 19, of which 15 were waited for; matrix products, arithmetic and copies ran while one was open for 24% of the time, Pallas kernels for 0%

profile of v1, /device:TPU:0, one launch (start us, length us, event | category | flops | bytes accessed | tf_op | source)
XLA Modules:
  0.0 409.8 jit_solution(17242743665083099985)
XLA Ops:
  9.4 1.0 copy.69
  10.4 1.8 convolution_convert_fusion.2
  12.3 3.0 collective-permute-start
  15.3 1.6 bitcast_dynamic-update-slice_fusion.15
  16.9 1.1 convolution_multiply_fusion.4
  19.7 41.6 %all-reduce = bf16[32]{0:T(256)(128)(2,1)S(1)} all-reduce(bf16[32]{0:T(256)(128)(2,1)S(1)} %dynamic-update-slice), channel_id=2, replica_groups=mesh['seq'=16,'head'=2] {'seq'}, use_global_device_ids=true, to_apply=%add | all-reduce | flops 32 | bytes 128
  62.1 10.0 %collective-permute-done.1 = bf16[256,256]{1,0:T(8,128)(2,1)S(1)} collective-permute-done((bf16[256,256]{1,0:T(8,128)(2,1)S(1)}, bf16[256,256]{1,0:T(8,128)(2,1)S(1)}, u32[]{:S(2)}, u32[]{:S(2)}) %collective-permute-start.1) | collective-permute-done | bytes 131104 | tf_op jit(solution)/shard_map/ppermute | solution.py:24
  72.8 7.9 %collective-permute-done.2 = bf16[256,256]{1,0:T(8,128)(2,1)S(1)} collective-permute-done((bf16[256,256]{1,0:T(8,128)(2,1)S(1)}, bf16[256,256]{1,0:T(8,128)(2,1)S(1)}, u32[]{:S(2)}, u32[]{:S(2)}) %collective-permute-start.2) | collective-permute-done | bytes 131104 | tf_op jit(solution)/shard_map/ppermute | solution.py:24
  81.3 8.0 %collective-permute-done.3 = bf16[256,256]{1,0:T(8,128)(2,1)S(1)} collective-permute-done((bf16[256,256]{1,0:T(8,128)(2,1)S(1)}, bf16[256,256]{1,0:T(8,128)(2,1)S(1)}, u32[]{:S(2)}, u32[]{:S(2)}) %collective-permute-start.3) | collective-permute-done | bytes 131104 | tf_op jit(solution)/shard_map/ppermute | solution.py:24
  90.0 8.3 %collective-permute-done.4 = bf16[256,256]{1,0:T(8,128)(2,1)S(1)} collective-permute-done((bf16[256,256]{1,0:T(8,128)(2,1)S(1)}, bf16[256,256]{1,0:T(8,128)(2,1)S(1)}, u32[]{:S(2)}, u32[]{:S(2)}) %collective-permute-start.4) | collective-permute-done | bytes 131104 | tf_op jit(solution)/shard_map/ppermute | solution.py:24
  99.0 9.7 %collective-permute-done.5 = bf16[256,256]{1,0:T(8,128)(2,1)S(1)} collective-permute-done((bf16[256,256]{1,0:T(8,128)(2,1)S(1)}, bf16[256,256]{1,0:T(8,128)(2,1)S(1)}, u32[]{:S(2)}, u32[]{:S(2)}) %collective-permute-start.5) | collective-permute-done | bytes 131104 | tf_op jit(solution)/shard_map/ppermute | solution.py:24
  109.4 8.1 %collective-permute-done.6 = bf16[256,256]{1,0:T(8,128)(2,1)S(1)} collective-permute-done((bf16[256,256]{1,0:T(8,128)(2,1)S(1)}, bf16[256,256]{1,0:T(8,128)(2,1)S(1)}, u32[]{:S(2)}, u32[]{:S(2)}) %collective-permute-start.6) | collective-permute-done | bytes 131104 | tf_op jit(solution)/shard_map/ppermute | solution.py:24
  118.2 10.9 %collective-permute-done.7 = bf16[256,256]{1,0:T(8,128)(2,1)S(1)} collective-permute-done((bf16[256,256]{1,0:T(8,128)(2,1)S(1)}, bf16[256,256]{1,0:T(8,128)(2,1)S(1)}, u32[]{:S(2)}, u32[]{:S(2)}) %collective-permute-start.7) | collective-permute-done | bytes 131104 | tf_op jit(solution)/shard_map/ppermute | solution.py:24
  129.8 10.6 %collective-permute-done.8 = bf16[256,256]{1,0:T(8,128)(2,1)S(1)} collective-permute-done((bf16[256,256]{1,0:T(8,128)(2,1)S(1)}, bf16[256,256]{1,0:T(8,128)(2,1)S(1)}, u32[]{:S(2)}, u32[]{:S(2)}) %collective-permute-start.8) | collective-permute-done | bytes 131104 | tf_op jit(solution)/shard_map/ppermute | solution.py:24
  141.1 7.9 %collective-permute-done.9 = bf16[256,256]{1,0:T(8,128)(2,1)S(1)} collective-permute-done((bf16[256,256]{1,0:T(8,128)(2,1)S(1)}, bf16[256,256]{1,0:T(8,128)(2,1)S(1)}, u32[]{:S(2)}, u32[]{:S(2)}) %collective-permute-start.9) | collective-permute-done | bytes 131104 | tf_op jit(solution)/shard_map/ppermute | solution.py:24
  149.7 7.9 %collective-permute-done.10 = bf16[256,256]{1,0:T(8,128)(2,1)S(1)} collective-permute-done((bf16[256,256]{1,0:T(8,128)(2,1)S(1)}, bf16[256,256]{1,0:T(8,128)(2,1)S(1)}, u32[]{:S(2)}, u32[]{:S(2)}) %collective-permute-start.10) | collective-permute-done | bytes 131104 | tf_op jit(solution)/shard_map/ppermute | solution.py:24
  158.2 7.9 %collective-permute-done.11 = bf16[256,256]{1,0:T(8,128)(2,1)S(1)} collective-permute-done((bf16[256,256]{1,0:T(8,128)(2,1)S(1)}, bf16[256,256]{1,0:T(8,128)(2,1)S(1)}, u32[]{:S(2)}, u32[]{:S(2)}) %collective-permute-start.11) | collective-permute-done | bytes 131104 | tf_op jit(solution)/shard_map/ppermute | solution.py:24
  166.8 7.9 %collective-permute-done.12 = bf16[256,256]{1,0:T(8,128)(2,1)S(1)} collective-permute-done((bf16[256,256]{1,0:T(8,128)(2,1)S(1)}, bf16[256,256]{1,0:T(8,128)(2,1)S(1)}, u32[]{:S(2)}, u32[]{:S(2)}) %collective-permute-start.12) | collective-permute-done | bytes 131104 | tf_op jit(solution)/shard_map/ppermute | solution.py:24
  175.3 7.9 %collective-permute-done.13 = bf16[256,256]{1,0:T(8,128)(2,1)S(1)} collective-permute-done((bf16[256,256]{1,0:T(8,128)(2,1)S(1)}, bf16[256,256]{1,0:T(8,128)(2,1)S(1)}, u32[]{:S(2)}, u32[]{:S(2)}) %collective-permute-start.13) | collective-permute-done | bytes 131104 | tf_op jit(solution)/shard_map/ppermute | solution.py:24
  183.9 7.9 %collective-permute-done.14 = bf16[256,256]{1,0:T(8,128)(2,1)S(1)} collective-permute-done((bf16[256,256]{1,0:T(8,128)(2,1)S(1)}, bf16[256,256]{1,0:T(8,128)(2,1)S(1)}, u32[]{:S(2)}, u32[]{:S(2)}) %collective-permute-start.14) | collective-permute-done | bytes 131104 | tf_op jit(solution)/shard_map/ppermute | solution.py:24
  192.5 3.6 gather_fusion
  196.1 4.0 reshape.197
  200.1 15.6 %while.39 = (s32[]{:T(128)}, f32[2,128,128]{2,1,0:T(8,128)S(1)}, s32[]{:T(128)}, bf16[16,2]{1,0:T(8,128)(2,1)S(1)}, bf16[16,2,128,128]{3,2,1,0:T(8,128)(2,1)}, /*index=5*/s32[]{:T(128)}, s32[]{:T(128)}) while((s32[]{:T(128)}, f32[2,128,128]{2,1,0:T(8,128)S(1)}, s32[]{:T(128)}, bf16[16,2]{1,0:T(8,128)(2,1)S(1)}, ...), condition=%wide.region_3.4_spmd.clone, body=%wide.region_2.3_spmd.clone.sunk | while | flops 163846 | bytes 327805 | solution.py:51
  200.1 1.0 fusion.79
  201.1 0.9 fusion.79
  203.0 0.9 fusion.79
  205.0 0.9 fusion.79
  216.5 2.0 convolution_convert_fusion.1
  218.7 4.0 reshape.196
  222.8 141.1 %while.38 = (s32[]{:T(128)}, f32[2,128]{1,0:T(2,128)S(1)}, f32[2,128]{1,0:T(2,128)S(1)}, f32[128,2,128]{2,0,1:T(8,128)S(1)}, f32[2,128]{1,0:T(2,128)S(1)}, /*ind...) while((s32[]{:T(128)}, f32[2,128]{1,0:T(2,128)S(1)}, ...), condition=%wide.region_23.24_spmd.clone.clone, body=%wide.region_6.23_spmd.clone.clone.sunk | while | flops 34162200 | bytes 2310995 | solution.py:170
  226.0 1.0 constant_dynamic-slice_fusion.3
  231.4 1.0 constant_dynamic-slice_fusion.3
  236.3 1.0 constant_dynamic-slice_fusion.3
  240.6 1.0 constant_dynamic-slice_fusion.3
  245.0 1.0 constant_dynamic-slice_fusion.3
  249.4 1.0 constant_dynamic-slice_fusion.3
  253.7 1.0 constant_dynamic-slice_fusion.3
  258.1 1.0 constant_dynamic-slice_fusion.3
  262.4 1.0 constant_dynamic-slice_fusion.3
  266.8 1.0 constant_dynamic-slice_fusion.3
  271.2 1.0 constant_dynamic-slice_fusion.3
  275.5 1.0 constant_dynamic-slice_fusion.3
  279.9 1.0 constant_dynamic-slice_fusion.3
  284.3 1.0 constant_dynamic-slice_fusion.3
  288.6 1.0 constant_dynamic-slice_fusion.3
  293.0 1.0 constant_dynamic-slice_fusion.3
  297.3 1.0 constant_dynamic-slice_fusion.3
  301.7 1.0 constant_dynamic-slice_fusion.3
  306.1 1.0 constant_dynamic-slice_fusion.3
  310.4 1.0 constant_dynamic-slice_fusion.3
  314.8 1.0 constant_dynamic-slice_fusion.3
  319.1 1.0 constant_dynamic-slice_fusion.3
  323.5 1.0 constant_dynamic-slice_fusion.3
  327.9 1.0 constant_dynamic-slice_fusion.3
  332.2 1.0 constant_dynamic-slice_fusion.3
  336.6 1.0 constant_dynamic-slice_fusion.3
  340.9 1.0 constant_dynamic-slice_fusion.3
  345.3 1.0 constant_dynamic-slice_fusion.3
  349.7 1.0 constant_dynamic-slice_fusion.3
  354.0 1.0 constant_dynamic-slice_fusion.3
  358.4 1.0 constant_dynamic-slice_fusion.3
  362.8 1.0 constant_dynamic-slice_fusion.3
  364.2 3.7 convolution_convert_fusion
  367.9 35.3 %reduce-scatter.5.cloned.1.call-done = bf16[256,2048]{1,0:T(8,128)(2,1)} async-done(((bf16[256,4096]{1,0:T(8,128)(2,1)}), bf16[256,2048]{1,0:T(8,128)(2,1)}) %reduce-scatter.5.cloned.1.call-update) | async-done | bytes 1048592 | tf_op jit(solution)/shard_map/reduce_scatter | solution.py:193
  (387 shorter events, 53.6 us)
Async XLA Ops:
  7.2 209.4 %copy-start = (bf16[256,4096]{1,0:T(8,128)(2,1)S(1)}, bf16[256,4096]{1,0:T(8,128)(2,1)}, u32[]{:S(2)}) copy-start(bf16[256,4096]{1,0:T(8,128)(2,1)} %param.28) | copy-start | bytes 6291460
  7.2 11.0 %copy-start.4 = (u32[32]{0:T(128)S(1)}, u32[32]{0:T(128)}, u32[]{:S(2)}) copy-start(u32[32]{0:T(128)} %constant.137) | copy-start | bytes 388
  7.2 10.9 %copy-start.2 = (bf16[256,256]{1,0:T(8,128)(2,1)S(1)}, bf16[256,256]{1,0:T(8,128)(2,1)}, u32[]{:S(2)}) copy-start(bf16[256,256]{1,0:T(8,128)(2,1)} %param.25) | copy-start | bytes 393220
  7.2 192.9 %all-gather.7.cloned.1.call-start = ((), (), s32[]{:S(2)}) async-start(), calls=%async_computation.5 | async-start | bytes 1114112 | tf_op jit(solution)/shard_map/all_gather | solution.py:34
  12.2 206.4 %all-gather.5.cloned.1.call-start = ((), (), s32[]{:S(2)}) async-start(), calls=%async_computation.3 | async-start | bytes 2228224 | tf_op jit(solution)/shard_map/all_gather | solution.py:152
  12.3 49.1 %collective-permute-start = (bf16[256,256]{1,0:T(8,128)(2,1)}, bf16[256,256]{1,0:T(8,128)(2,1)S(1)}, u32[]{:S(2)}, u32[]{:S(2)}) collective-permute-start(bf16[256,256]{1,0:T(8,128)(2,1)} %param.27), channel_id=1, source_target_pairs={{0,2},{2,4},{4,6},{6,8},{8,10},{10,12},{12,14},{14,16},{16,18},{18... | collective-permute-start | bytes 393224 | tf_op jit(solution)/shard_map/ppermute | solution.py:24
  15.3 352.6 %reduce-scatter.3.cloned.1.call-start = ((), (), s32[]{:S(2)}) async-start(), calls=%async_computation.2 | async-start | bytes 3145728 | tf_op jit(solution)/shard_map/reduce_scatter | solution.py:187
  61.4 10.7 %collective-permute-start.1 = (bf16[256,256]{1,0:T(8,128)(2,1)S(1)}, bf16[256,256]{1,0:T(8,128)(2,1)S(1)}, u32[]{:S(2)}, u32[]{:S(2)}) collective-permute-start(bf16[256,256]{1,0:T(8,128)(2,1)S(1)} %collective-permute-done), channel_id=1, source_target_pairs={{0,2},{2,4},{4,6},{6,8},{8,10},{10,12},{12,14},{14,16},{16,18},{18... | collective-permute-start | bytes 393224 | tf_op jit(solution)/shard_map/ppermute | solution.py:24
  72.1 8.6 %collective-permute-start.2 = (bf16[256,256]{1,0:T(8,128)(2,1)S(1)}, bf16[256,256]{1,0:T(8,128)(2,1)S(1)}, u32[]{:S(2)}, u32[]{:S(2)}) collective-permute-start(bf16[256,256]{1,0:T(8,128)(2,1)S(1)} %collective-permute-done.1), channel_id=1, source_target_pairs={{0,2},{2,4},{4,6},{6,8},{8,10},{10,12},{12,14},{14,16},{16,18},{18... | collective-permute-start | bytes 393224 | tf_op jit(solution)/shard_map/ppermute | solution.py:24
  80.7 8.7 %collective-permute-start.3 = (bf16[256,256]{1,0:T(8,128)(2,1)S(1)}, bf16[256,256]{1,0:T(8,128)(2,1)S(1)}, u32[]{:S(2)}, u32[]{:S(2)}) collective-permute-start(bf16[256,256]{1,0:T(8,128)(2,1)S(1)} %collective-permute-done.2), channel_id=1, source_target_pairs={{0,2},{2,4},{4,6},{6,8},{8,10},{10,12},{12,14},{14,16},{16,18},{18... | collective-permute-start | bytes 393224 | tf_op jit(solution)/shard_map/ppermute | solution.py:24
  89.4 9.0 %collective-permute-start.4 = (bf16[256,256]{1,0:T(8,128)(2,1)S(1)}, bf16[256,256]{1,0:T(8,128)(2,1)S(1)}, u32[]{:S(2)}, u32[]{:S(2)}) collective-permute-start(bf16[256,256]{1,0:T(8,128)(2,1)S(1)} %collective-permute-done.3), channel_id=1, source_target_pairs={{0,2},{2,4},{4,6},{6,8},{8,10},{10,12},{12,14},{14,16},{16,18},{18... | collective-permute-start | bytes 393224 | tf_op jit(solution)/shard_map/ppermute | solution.py:24
  98.3 10.4 %collective-permute-start.5 = (bf16[256,256]{1,0:T(8,128)(2,1)S(1)}, bf16[256,256]{1,0:T(8,128)(2,1)S(1)}, u32[]{:S(2)}, u32[]{:S(2)}) collective-permute-start(bf16[256,256]{1,0:T(8,128)(2,1)S(1)} %collective-permute-done.4), channel_id=1, source_target_pairs={{0,2},{2,4},{4,6},{6,8},{8,10},{10,12},{12,14},{14,16},{16,18},{18... | collective-permute-start | bytes 393224 | tf_op jit(solution)/shard_map/ppermute | solution.py:24
  108.7 8.8 %collective-permute-start.6 = (bf16[256,256]{1,0:T(8,128)(2,1)S(1)}, bf16[256,256]{1,0:T(8,128)(2,1)S(1)}, u32[]{:S(2)}, u32[]{:S(2)}) collective-permute-start(bf16[256,256]{1,0:T(8,128)(2,1)S(1)} %collective-permute-done.5), channel_id=1, source_target_pairs={{0,2},{2,4},{4,6},{6,8},{8,10},{10,12},{12,14},{14,16},{16,18},{18... | collective-permute-start | bytes 393224 | tf_op jit(solution)/shard_map/ppermute | solution.py:24
  117.5 11.6 %collective-permute-start.7 = (bf16[256,256]{1,0:T(8,128)(2,1)S(1)}, bf16[256,256]{1,0:T(8,128)(2,1)S(1)}, u32[]{:S(2)}, u32[]{:S(2)}) collective-permute-start(bf16[256,256]{1,0:T(8,128)(2,1)S(1)} %collective-permute-done.6), channel_id=1, source_target_pairs={{0,2},{2,4},{4,6},{6,8},{8,10},{10,12},{12,14},{14,16},{16,18},{18... | collective-permute-start | bytes 393224 | tf_op jit(solution)/shard_map/ppermute | solution.py:24
  129.1 11.3 %collective-permute-start.8 = (bf16[256,256]{1,0:T(8,128)(2,1)S(1)}, bf16[256,256]{1,0:T(8,128)(2,1)S(1)}, u32[]{:S(2)}, u32[]{:S(2)}) collective-permute-start(bf16[256,256]{1,0:T(8,128)(2,1)S(1)} %collective-permute-done.7), channel_id=1, source_target_pairs={{0,2},{2,4},{4,6},{6,8},{8,10},{10,12},{12,14},{14,16},{16,18},{18... | collective-permute-start | bytes 393224 | tf_op jit(solution)/shard_map/ppermute | solution.py:24
  140.4 8.6 %collective-permute-start.9 = (bf16[256,256]{1,0:T(8,128)(2,1)S(1)}, bf16[256,256]{1,0:T(8,128)(2,1)S(1)}, u32[]{:S(2)}, u32[]{:S(2)}) collective-permute-start(bf16[256,256]{1,0:T(8,128)(2,1)S(1)} %collective-permute-done.8), channel_id=1, source_target_pairs={{0,2},{2,4},{4,6},{6,8},{8,10},{10,12},{12,14},{14,16},{16,18},{18... | collective-permute-start | bytes 393224 | tf_op jit(solution)/shard_map/ppermute | solution.py:24
  149.0 8.6 %collective-permute-start.10 = (bf16[256,256]{1,0:T(8,128)(2,1)S(1)}, bf16[256,256]{1,0:T(8,128)(2,1)S(1)}, u32[]{:S(2)}, u32[]{:S(2)}) collective-permute-start(bf16[256,256]{1,0:T(8,128)(2,1)S(1)} %collective-permute-done.9), channel_id=1, source_target_pairs={{0,2},{2,4},{4,6},{6,8},{8,10},{10,12},{12,14},{14,16},{16,18},{18... | collective-permute-start | bytes 393224 | tf_op jit(solution)/shard_map/ppermute | solution.py:24
  157.5 8.6 %collective-permute-start.11 = (bf16[256,256]{1,0:T(8,128)(2,1)S(1)}, bf16[256,256]{1,0:T(8,128)(2,1)S(1)}, u32[]{:S(2)}, u32[]{:S(2)}) collective-permute-start(bf16[256,256]{1,0:T(8,128)(2,1)S(1)} %collective-permute-done.10), channel_id=1, source_target_pairs={{0,2},{2,4},{4,6},{6,8},{8,10},{10,12},{12,14},{14,16},{16,18},{18... | collective-permute-start | bytes 393224 | tf_op jit(solution)/shard_map/ppermute | solution.py:24
  166.1 8.6 %collective-permute-start.12 = (bf16[256,256]{1,0:T(8,128)(2,1)S(1)}, bf16[256,256]{1,0:T(8,128)(2,1)S(1)}, u32[]{:S(2)}, u32[]{:S(2)}) collective-permute-start(bf16[256,256]{1,0:T(8,128)(2,1)S(1)} %collective-permute-done.11), channel_id=1, source_target_pairs={{0,2},{2,4},{4,6},{6,8},{8,10},{10,12},{12,14},{14,16},{16,18},{18... | collective-permute-start | bytes 393224 | tf_op jit(solution)/shard_map/ppermute | solution.py:24
  174.7 8.6 %collective-permute-start.13 = (bf16[256,256]{1,0:T(8,128)(2,1)S(1)}, bf16[256,256]{1,0:T(8,128)(2,1)S(1)}, u32[]{:S(2)}, u32[]{:S(2)}) collective-permute-start(bf16[256,256]{1,0:T(8,128)(2,1)S(1)} %collective-permute-done.12), channel_id=1, source_target_pairs={{0,2},{2,4},{4,6},{6,8},{8,10},{10,12},{12,14},{14,16},{16,18},{18... | collective-permute-start | bytes 393224 | tf_op jit(solution)/shard_map/ppermute | solution.py:24
  183.2 8.6 %collective-permute-start.14 = (bf16[256,256]{1,0:T(8,128)(2,1)S(1)}, bf16[256,256]{1,0:T(8,128)(2,1)S(1)}, u32[]{:S(2)}, u32[]{:S(2)}) collective-permute-start(bf16[256,256]{1,0:T(8,128)(2,1)S(1)} %collective-permute-done.13), channel_id=1, source_target_pairs={{0,2},{2,4},{4,6},{6,8},{8,10},{10,12},{12,14},{14,16},{16,18},{18... | collective-permute-start | bytes 393224 | tf_op jit(solution)/shard_map/ppermute | solution.py:24
  196.1 19.6 %copy-start.3 = (bf16[256,256]{1,0:T(8,128)(2,1)S(1)}, bf16[256,256]{1,0:T(8,128)(2,1)}, u32[]{:S(2)}) copy-start(bf16[256,256]{1,0:T(8,128)(2,1)} %param.21) | copy-start | bytes 393220
  200.1 15.9 %copy-start.1 = (bf16[256,256]{1,0:T(8,128)(2,1)S(1)}, bf16[256,256]{1,0:T(8,128)(2,1)}, u32[]{:S(2)}) copy-start(bf16[256,256]{1,0:T(8,128)(2,1)} %param.23) | copy-start | bytes 393220
  218.6 184.6 %reduce-scatter.5.cloned.1.call-start = ((), (), s32[]{:S(2)}) async-start(), calls=%async_computation.4 | async-start | bytes 3145728 | tf_op jit(solution)/shard_map/reduce_scatter | solution.py:193
Sparse Core Ops, SparseCore 0:
  12.3 60.3 all-gather.6
  75.5 65.1 all-gather.4
  218.7 5.4 reduce-scatter.2
  368.0 35.1 reduce-scatter.4
